TPU v7x, 512 devices: a whole 4x4x16 slice. The times are simulated.
512 devices in a mesh: wide: 128 (over z, y, core), narrow: 4 (over x).
Axes of the slice: x: 4, y: 4, z: 16, core: 2. Of those that a mesh axis runs over, the one named last changes fastest.
Arguments:
- sketch: float32 [64, 65536], P(None, ('wide', 'narrow')), may hold values from -1000 to 1000
- ppmi_slab: float32 [4096, 65536], P('wide', 'narrow'), may hold values from 0 to 8
Outputs:
- orthonormal: float32 [64, 65536], P(None, ('wide', 'narrow'))
- projected: float32 [64, 65536], P(None, ('narrow', 'wide'))
All inputs are finite; a program needn't handle non-finite values.
Results may differ from a plain program's by a relative error of at most 0.000076.
Values sent between devices are 32-bit elements; how exact they have to be, the bound alone decides.
No kernel may reach another device: no remote copies, remote signals or barrier semaphores. Data moves between devices by JAX's collectives and lax.ppermute only.
A program may use at most 64 MiB of HBM per device.

v0:
```python
import math

import jax
import jax.numpy as jnp
from jax import lax
from jax.sharding import PartitionSpec as P

SUB = 8


def local(sketch, ppmi_slab):
    rows_total = sketch.shape[1] * lax.axis_size("wide") * lax.axis_size("narrow")
    slab_rows = SUB * lax.axis_size("wide") * lax.axis_size("narrow")
    scaling = 1.0 / math.sqrt(slab_rows)
    local_gram = jnp.dot(sketch, sketch.T, precision=lax.Precision.HIGHEST) / rows_total
    gram_matrix = lax.psum(local_gram, ("wide", "narrow"))
    lower_factor = jnp.linalg.cholesky(gram_matrix)
    orthonormal = lax.linalg.triangular_solve(lower_factor, sketch, left_side=True, lower=True)
    picked = lax.all_gather(orthonormal[:, :SUB], "narrow", axis=1, tiled=True)
    partial_value = jnp.dot(picked, ppmi_slab, precision=lax.Precision.HIGHEST)
    summed = lax.psum_scatter(partial_value, "wide", scatter_dimension=1, tiled=True)
    projected = summed * scaling
    return (orthonormal, projected)


def solution(mesh):
    placed = (P(None, ("wide", "narrow")), P("wide", "narrow"))
    return jax.shard_map(
        local,
        mesh=mesh,
        in_specs=placed,
        out_specs=(P(None, ("wide", "narrow")), P(None, ("narrow", "wide"))),
        check_vma=False,
    )
```

profile of v0, /device:TPU:6, one launch (start us, length us, event | category | flops | bytes accessed | tf_op | source)
XLA Modules:
  0.0 415.4 jit_solution(18011098815366925033)
XLA Ops:
  7.2 0.0 copy-start
  7.2 0.0 reduce-scatter.2.cloned.1.call-start
  7.2 1.1 convolution_multiply_fusion
  8.3 108.5 %psum.7 = f32[64,64]{0,1:T(8,128)S(1)} all-reduce(f32[64,64]{0,1:T(8,128)S(1)} %convolution_multiply_fusion), channel_id=1, replica_groups=mesh['wide'=128,'narrow'=4] {'wide','narrow'}, use_global_device_ids=true, to_apply=%region_0.0 | all-reduce | flops 4096 | bytes 32768 | tf_op jit(solution)/shard_map/psum | solution.py:16
  116.8 0.1 copy.7
  116.9 5.8 %cholesky.16 = f32[64,64]{1,0:T(8,128)S(1)} custom-call(f32[64,64]{1,0:T(8,128)S(1)} %fusion.3), custom_call_target="Cholesky" | custom-call | tf_op jit(solution)/shard_map/jit(cholesky)/cholesky | solution.py:17
  122.8 0.6 compare_reduce_fusion
  123.4 0.7 fusion
  124.1 4.9 %custom-call.6 = f32[1,64,64]{1,2,0:T(8,128)S(1)} custom-call(f32[1,64,64]{2,1,0:T(8,128)S(1)} %fusion), custom_call_target="InvertDiagBlocksLowerTriangular" | custom-call | tf_op jit(solution)/shard_map/triangular_solve | solution.py:18
  129.0 1.0 fusion.1
  130.0 0.0 copy-start.1
  130.0 0.1 copy.8
  130.1 11.9 %all_gather.3 = f32[64,32]{0,1:T(8,128)S(1)} all-gather(f32[64,8]{0,1:T(8,128)S(1)} %copy.8), channel_id=1, replica_groups=mesh['wide'=128,'narrow'=4] {'narrow'}, dimensions={1}, use_global_device_ids=true | all-gather | bytes 10240 | tf_op jit(solution)/shard_map/all_gather | solution.py:19
  142.0 0.0 copy-done
  142.0 5.0 %fusion.4 = f32[64,16384]{1,0:T(8,128)} fusion(f32[64,32]{0,1:T(8,128)S(1)} %all_gather.3, f32[32,16384]{1,0:T(8,128)S(1)} %copy-done), kind=kOutput, calls=%fused_computation.12 | convolution fusion | flops 402653184 | bytes 6299648 | tf_op jit(solution)/shard_map/dot_general | solution.py:20
  147.0 0.0 copy-done.1
  147.0 0.0 reduce-scatter.2.cloned.1.call-update
  147.1 260.1 %reduce-scatter.2.cloned.1.call-done = f32[64,128]{1,0:T(8,128)} async-done(((f32[64,16384]{1,0:T(8,128)}), f32[64,128]{1,0:T(8,128)}) %reduce-scatter.2.cloned.1.call-update) | async-done | bytes 32784 | tf_op jit(solution)/shard_map/reduce_scatter | solution.py:21
  407.2 1.4 broadcast_multiply_fusion
  (2 shorter events, 0.0 us)
Async XLA Ops:
  7.2 134.9 %copy-start = (f32[32,16384]{1,0:T(8,128)S(1)}, f32[32,16384]{1,0:T(8,128)}, u32[]{:S(2)}) copy-start(f32[32,16384]{1,0:T(8,128)} %param.3) | copy-start | bytes 6291460
  7.2 400.0 %reduce-scatter.2.cloned.1.call-start = ((), (), s32[]{:S(2)}) async-start(), calls=%async_computation.1 | async-start | bytes 4227072 | tf_op jit(solution)/shard_map/reduce_scatter | solution.py:21
  130.0 17.0 %copy-start.1 = (f32[64,128]{1,0:T(8,128)}, f32[64,128]{1,0:T(8,128)S(1)}, u32[]{:S(2)}) copy-start(f32[64,128]{1,0:T(8,128)S(1)} %fusion.1) | copy-start | bytes 98308
Sparse Core Ops, SparseCore 0:
  147.2 259.9 reduce-scatter.1
where the time goes:
time: 416 us; the launch traced here: 415 us
  waiting for transfers between devices  260 us (62%)
  blocking collectives  120 us (29%)
  between operations  14.1 us (3%)
  other arithmetic  13.5 us (3%)
  matrix products  7.11 us (2%)
    reduce_scatter x1, waiting for transfers between devices, local(): lax.psum_scatter(partial_value, 'wide', scatter_dimension=1, tiled=True)  260 us
    psum x1, blocking collectives, local(): gram_matrix = lax.psum(local_gram, ('wide', 'narrow'))  108 us
    all_gather x1, blocking collectives, local(): picked = lax.all_gather(orthonormal[:, :SUB], 'narrow', axis=1, tiled=True)  11.9 us
  transfers between devices with their start and end apart: 1, of which 1 were waited for; matrix products, arithmetic and copies ran while one was open for 0% of the time, Pallas kernels for 0%

commit v1 on v0

v1 whole, which is shorter than its diff:
```python
import jax
import jax.numpy as jnp
from jax import lax
from jax.sharding import Mesh, PartitionSpec as P

SUB = 8
HI = lax.Precision.HIGHEST


def local(sketch, slab):
    k, sk = sketch.shape
    nz, ny, nc, nx = (lax.axis_size(a) for a in ("z", "y", "c", "x"))
    rows, cols = slab.shape
    out = cols // (nz * ny * nc)
    y, c = lax.axis_index("y"), lax.axis_index("c")
    blocks = slab.reshape(rows, nz, ny, nc * out)
    sent = []
    for d in range(ny):
        piece = lax.dynamic_index_in_dim(blocks, lax.rem(y + d, ny), 2, keepdims=False)
        if d:
            piece = lax.ppermute(piece, "y", [(i, (i + d) % ny) for i in range(ny)])
        sent.append(piece)

    gram = jnp.dot(sketch, sketch.T, precision=HI) / (sk * nz * ny * nc * nx)
    own = jnp.concatenate([sketch[:, :SUB].T, gram], axis=0)
    got = lax.all_to_all(jnp.broadcast_to(own, (nx, *own.shape)), "x", 0, 0, tiled=True)
    sel = got[:, :SUB].reshape(nx * SUB, k)
    own = jnp.concatenate([sel, got[:, SUB:].sum(0)], axis=0)
    got = lax.all_to_all(jnp.broadcast_to(own, (ny * nc, *own.shape)), ("y", "c"), 0, 0, tiled=True)
    sel = got[:, :rows].reshape(ny, nc, rows, k)
    gram = got[:, rows:].sum(0)

    sel = lax.dynamic_index_in_dim(sel, c, 1, keepdims=False)
    part = 0.0
    for d in range(ny):
        s = lax.dynamic_index_in_dim(sel, lax.rem(y - d + ny, ny), 0, keepdims=False)
        part += lax.dot_general(s, sent[d].reshape(rows, nz * nc * out), (((0,), (0,)), ((), ())), precision=HI)
    part = part.reshape(k, nz, nc, out)
    keep = lax.dynamic_index_in_dim(part, c, 2, keepdims=False)
    away = lax.dynamic_index_in_dim(part, 1 - c, 2, keepdims=False)
    part = keep + lax.ppermute(away, "c", [(0, 1), (1, 0)])

    part = part.transpose(1, 0, 2)
    gram = jnp.broadcast_to(gram.reshape(-1, out), (nz, k * k // out, out))
    got = lax.all_to_all(jnp.concatenate([part, gram], axis=1), "z", 0, 0, tiled=True).sum(0)
    gram = got[k:].reshape(k, k)
    lower = jnp.linalg.cholesky(gram)
    both = jnp.concatenate([sketch, got[:k]], axis=1)
    both = lax.linalg.triangular_solve(lower, both, left_side=True, lower=True)
    total = rows * nz * ny * nc
    return both[:, :sk], both[:, sk:] * (1.0 / total**0.5)


def solution(mesh):
    nx = mesh.shape["narrow"]
    grid = Mesh(mesh.devices.reshape(-1, 4, 2, nx), ("z", "y", "c", "x"))
    return jax.shard_map(
        local,
        mesh=grid,
        in_specs=(P(None, ("z", "y", "c", "x")), P(("z", "y", "c"), "x")),
        out_specs=(P(None, ("z", "y", "c", "x")), P(None, ("x", "z", "y", "c"))),
        check_vma=False,
    )
```

time: 416 us -> 130 us (0.31)
  waiting for transfers between devices: 260 us -> 13.4 us
  blocking collectives: 120 us -> 55.9 us
  starting transfers between devices: 0.04 us -> 24.8 us
  local copies, waits for them, and re-layouts: 0.15 us -> 13.8 us
  between operations: 14.1 us -> 0.95 us
    reduce_scatter x1 -> x0, waiting for transfers between devices: 260 us -> none  [local(): lax.psum_scatter(partial_value, 'wide', scatter_dimension=1, tiled=True)]
    psum x1 -> x0, blocking collectives: 108 us -> none  [local(): gram_matrix = lax.psum(local_gram, ('wide', 'narrow'))]
    all_to_all x0 -> x1, blocking collectives: none -> 55.9 us  [local(): lax.all_to_all(jnp.concatenate([part, gram], axis=1), 'z', 0, 0, tiled=True)]
    all_to_all x0 -> x2, starting transfers between devices: none -> 13.9 us  [the longest x1 9.15 us: local(): lax.all_to_all(jnp.broadcast_to(own, (nx, *own.shape)), 'x', 0, 0, tiled=...]
    all_gather x1 -> x0, blocking collectives: 11.9 us -> none  [local(): picked = lax.all_gather(orthonormal[:, :SUB], 'narrow', axis=1, tiled=True)]
    all_to_all x0 -> x2, waiting for transfers between devices: none -> 11.8 us  [the longest x1 11.8 us: local(): lax.all_to_all(jnp.broadcast_to(own, (ny * nc, *own.shape)), ('y', 'c'),...]
    ppermute x0 -> x4, starting transfers between devices: none -> 10.9 us  [the longest x3 8.96 us: local(): piece = lax.ppermute(piece, 'y', [(i, (i + d) % ny) for i in range(ny)])]
    dynamic_slice x0 -> x3, local copies, waits for them, and re-layouts: none -> 4.37 us  [the longest x1 3.12 us: local(): lax.dynamic_index_in_dim(blocks, lax.rem(y + d, ny), 2, keepdims=False)]
  transfers between devices with their start and end apart: 1 -> 6, of which waited for: 1 -> 2; matrix products, arithmetic and copies ran while one was open for 0% -> 8% of each run, Pallas kernels for 0% -> 0%
where the time goes in v1:
time: 130 us; the launch traced here: 127 us
  blocking collectives  55.9 us (43%)
  starting transfers between devices  24.8 us (19%)
  local copies, waits for them, and re-layouts  13.8 us (11%)
  other arithmetic  13.4 us (10%)
  waiting for transfers between devices  13.4 us (10%)
  matrix products  5.16 us (4%)
    all_to_all x1, blocking collectives, local(): lax.all_to_all(jnp.concatenate([part, gram], axis=1), 'z', 0, 0, tiled=True)  55.9 us
    all_to_all x1, waiting for transfers between devices, local(): lax.all_to_all(jnp.broadcast_to(own, (ny * nc, *own.shape)), ('y', 'c'),...  11.8 us
    all_to_all x1, starting transfers between devices, local(): lax.all_to_all(jnp.broadcast_to(own, (nx, *own.shape)), 'x', 0, 0, tiled=...  9.15 us
    ppermute x3, starting transfers between devices, local(): piece = lax.ppermute(piece, 'y', [(i, (i + d) % ny) for i in range(ny)])  8.96 us
    another operation x3, other arithmetic, local(): lower = jnp.linalg.cholesky(gram)  6.52 us
    another operation x2, other arithmetic, local(): both = lax.linalg.triangular_solve(lower, both, left_side=True, lower=True)  5.55 us
    all_to_all x1, starting transfers between devices, local(): lax.all_to_all(jnp.broadcast_to(own, (ny * nc, *own.shape)), ('y', 'c'),...  4.79 us
    dot_general x4, matrix products, local(): lax.dot_general(s, sent[d].reshape(rows, nz * nc * out), (((0,), (0,)), (...  3.9 us
  transfers between devices with their start and end apart: 6, of which 2 were waited for; matrix products, arithmetic and copies ran while one was open for 8% of the time, Pallas kernels for 0%

profile of v1, /device:TPU:6, one launch (start us, length us, event | category | flops | bytes accessed | tf_op | source)
XLA Modules:
  0.0 127.4 jit_solution(9438784963353973848)
XLA Ops:
  0.6 1.0 convolution_multiply_fusion
  1.7 0.8 slice_bitcast_fusion
  2.4 0.1 pad_maximum_fusion.1
  2.5 0.7 broadcast_in_dim.11
  3.2 9.1 %all-to-all-start = ((f32[4,72,64]{1,2,0:T(8,128)}), f32[4,72,64]{1,2,0:T(8,128)S(1)}, u32[]{:S(2)}, u32[]{:S(2)}) async-start(f32[4,72,64]{1,2,0:T(8,128)} %broadcast_in_dim.11), calls=%async_computation | async-start | bytes 262144 | tf_op jit(solution)/shard_map/all_to_all | solution.py:26
  12.3 2.7 %reshape.54 = f32[32,16,4,256]{3,2,1,0:T(4,128)S(1)} reshape(f32[32,16384]{1,0:T(8,128)} %param.3) | data formatting | bytes 4194304 | tf_op jit(solution)/shard_map/reshape | solution.py:16
  15.0 3.1 %constant_dynamic-slice_fusion.3 = (f32[32,16,1,256]{3,2,1,0:T(1,128)S(1)}, f32[32,16,1,256]{3,2,1,0:T(1,128)S(1)}, f32[32,16,1,256]{3,2,1,0:T(1,128)S(1)}, f32[32,16,256]{2,1,0:T(8,128)S(1)}) fusion(f32[32,16,4,256]{3,2,1,0:T(4,128)S(1)} %reshape.54, s32[]{:T(128)S(6)} %select_n.51, s32[]{:T(128)S(6)} %select_n.48, s32[]{:T(128)S(6)} %select_n.50, ...), kind=kLoop, calls=%fused_computation.44 | loop fusion | bytes 4194320 | tf_op jit(solution)/shard_map/jit(dynamic_index_in_dim)/dynamic_slice | solution.py:19
  18.2 1.9 %collective-permute-start = (f32[32,16,256]{2,1,0:T(8,128)S(1)}, f32[32,16,256]{2,1,0:T(8,128)S(1)}, u32[]{:S(2)}, u32[]{:S(2)}) collective-permute-start(f32[32,16,256]{2,1,0:T(8,128)S(1)} %bitcast.69), channel_id=1, source_target_pairs={{0,8},{8,16},{16,24},{24,0},{1,9},{9,17},{17,25},{25,1},{2,10},{10... | collective-permute-start | bytes 1572872 | tf_op jit(solution)/shard_map/ppermute | solution.py:21
  20.1 5.1 %collective-permute-start.2 = (f32[32,16,256]{2,1,0:T(8,128)S(1)}, f32[32,16,256]{2,1,0:T(8,128)S(1)}, u32[]{:S(2)}, u32[]{:S(2)}) collective-permute-start(f32[32,16,256]{2,1,0:T(8,128)S(1)} %bitcast.71), channel_id=1, source_target_pairs={{0,24},{8,0},{16,8},{24,16},{1,25},{9,1},{17,9},{25,17},{2,26},{10... | collective-permute-start | bytes 1572872 | tf_op jit(solution)/shard_map/ppermute | solution.py:21
  25.3 0.8 copy.41
  26.1 1.9 %collective-permute-start.1 = (f32[32,16,256]{2,1,0:T(8,128)}, f32[32,16,256]{2,1,0:T(8,128)}, u32[]{:S(2)}, u32[]{:S(2)}) collective-permute-start(f32[32,16,256]{2,1,0:T(8,128)} %bitcast.54), channel_id=1, source_target_pairs={{0,16},{8,24},{16,0},{24,8},{1,17},{9,25},{17,1},{25,9},{2,18},{10... | collective-permute-start | bytes 1572872 | tf_op jit(solution)/shard_map/ppermute | solution.py:21
  28.0 0.0 all-to-all-done
  28.0 0.1 copy.30
  28.1 0.1 copy.22
  28.2 0.1 slice_reduce_fusion.1
  28.3 0.1 pad_maximum_fusion.2
  28.4 0.7 broadcast_in_dim.12
  29.1 4.8 %all-to-all-start.1 = ((f32[8,96,64]{1,2,0:T(8,128)}), f32[8,96,64]{1,2,0:T(8,128)S(1)}, u32[]{:S(2)}, u32[]{:S(2)}) async-start(f32[8,96,64]{1,2,0:T(8,128)} %broadcast_in_dim.12), calls=%async_computation.1 | async-start | bytes 524288 | tf_op jit(solution)/shard_map/all_to_all | solution.py:29
  33.9 0.3 copy.31
  34.3 11.8 %all-to-all-done.1 = f32[8,96,64]{1,2,0:T(8,128)S(1)} async-done(((f32[8,96,64]{1,2,0:T(8,128)}), f32[8,96,64]{1,2,0:T(8,128)S(1)}, u32[]{:S(2)}, u32[]{:S(2)}) %all-to-all-start.1) | async-done | bytes 196640 | tf_op jit(solution)/shard_map/all_to_all | solution.py:29
  46.1 1.0 fusion.13
  47.0 0.3 copy.32
  47.4 0.3 copy.34
  47.7 1.3 %copy.33 = f32[4,8,16,256]{3,1,2,0:T(8,128)S(1)} copy(f32[4,8,16,256]{3,2,1,0:T(8,128)} %bitcast.20) | data formatting | bytes 1048576
  49.0 1.0 fusion.9
  50.0 1.0 convolution_add_fusion.1
  51.0 1.0 fusion
  52.0 0.9 reshape.59
  52.9 1.1 constant_dynamic-slice_fusion.1
  54.0 0.2 copy.43
  54.2 1.9 %collective-permute-start.3 = (f32[64,16,128]{2,0,1:T(8,128)S(1)}, f32[64,16,128]{2,0,1:T(8,128)S(1)}, u32[]{:S(2)}, u32[]{:S(2)}) collective-permute-start(f32[64,16,128]{2,0,1:T(8,128)S(1)} %bitcast.73), channel_id=1, source_target_pairs={{0,4},{4,0},{1,5},{5,1},{2,6},{6,2},{3,7},{7,3},{8,12},{12,8},{9,1... | collective-permute-start | bytes 1572872 | tf_op jit(solution)/shard_map/ppermute | solution.py:41
  56.1 0.1 slice_reduce_fusion
  56.2 0.1 copy.25
  56.3 0.1 reshape.60
  56.4 1.6 %collective-permute-done.3 = f32[64,16,128]{2,0,1:T(8,128)S(1)} collective-permute-done((f32[64,16,128]{2,0,1:T(8,128)S(1)}, f32[64,16,128]{2,0,1:T(8,128)S(1)}, u32[]{:S(2)}, u32[]{:S(2)}) %collective-permute-start.3) | collective-permute-done | bytes 524320 | tf_op jit(solution)/shard_map/ppermute | solution.py:41
  58.0 0.2 fusion.1
  58.2 0.0 copy-start
  58.2 0.1 pad_maximum_fusion
  58.3 55.9 %all_to_all.15 = f32[16,96,128]{2,1,0:T(8,128)S(1)} all-to-all(f32[16,96,128]{2,1,0:T(8,128)S(1)} %pad_maximum_fusion), channel_id=1, replica_groups=mesh['z'=16,'y'=4,'c'=2,'x'=4] {'z'}, dimensions={0} | all-to-all | bytes 1572864 | tf_op jit(solution)/shard_map/all_to_all | solution.py:45
  114.2 0.1 reshape.61
  114.3 0.1 copy.26
  114.4 5.8 %cholesky.16 = f32[64,64]{1,0:T(8,128)S(1)} custom-call(f32[64,64]{1,0:T(8,128)S(1)} %fusion.8), custom_call_target="Cholesky" | custom-call | tf_op jit(solution)/shard_map/jit(cholesky)/cholesky | solution.py:47
  120.3 0.6 compare_reduce_fusion
  120.9 0.7 fusion.6
  121.6 4.9 %custom-call.6 = f32[1,64,64]{1,2,0:T(8,128)S(1)} custom-call(f32[1,64,64]{2,1,0:T(8,128)S(1)} %fusion.6), custom_call_target="InvertDiagBlocksLowerTriangular" | custom-call | tf_op jit(solution)/shard_map/triangular_solve | solution.py:49
  126.5 0.0 copy-done
  126.5 0.3 fusion.2
  126.8 0.6 slice_multiply_fusion
  (11 shorter events, 0.2 us)
Async XLA Ops:
  3.2 24.9 %all-to-all-start = ((f32[4,72,64]{1,2,0:T(8,128)}), f32[4,72,64]{1,2,0:T(8,128)S(1)}, u32[]{:S(2)}, u32[]{:S(2)}) async-start(f32[4,72,64]{1,2,0:T(8,128)} %broadcast_in_dim.11), calls=%async_computation | async-start | bytes 262144 | tf_op jit(solution)/shard_map/all_to_all | solution.py:26
  18.2 28.9 %collective-permute-start = (f32[32,16,256]{2,1,0:T(8,128)S(1)}, f32[32,16,256]{2,1,0:T(8,128)S(1)}, u32[]{:S(2)}, u32[]{:S(2)}) collective-permute-start(f32[32,16,256]{2,1,0:T(8,128)S(1)} %bitcast.69), channel_id=1, source_target_pairs={{0,8},{8,16},{16,24},{24,0},{1,9},{9,17},{17,25},{25,1},{2,10},{10... | collective-permute-start | bytes 1572872 | tf_op jit(solution)/shard_map/ppermute | solution.py:21
  20.1 27.2 %collective-permute-start.2 = (f32[32,16,256]{2,1,0:T(8,128)S(1)}, f32[32,16,256]{2,1,0:T(8,128)S(1)}, u32[]{:S(2)}, u32[]{:S(2)}) collective-permute-start(f32[32,16,256]{2,1,0:T(8,128)S(1)} %bitcast.71), channel_id=1, source_target_pairs={{0,24},{8,0},{16,8},{24,16},{1,25},{9,1},{17,9},{25,17},{2,26},{10... | collective-permute-start | bytes 1572872 | tf_op jit(solution)/shard_map/ppermute | solution.py:21
  26.1 21.6 %collective-permute-start.1 = (f32[32,16,256]{2,1,0:T(8,128)}, f32[32,16,256]{2,1,0:T(8,128)}, u32[]{:S(2)}, u32[]{:S(2)}) collective-permute-start(f32[32,16,256]{2,1,0:T(8,128)} %bitcast.54), channel_id=1, source_target_pairs={{0,16},{8,24},{16,0},{24,8},{1,17},{9,25},{17,1},{25,9},{2,18},{10... | collective-permute-start | bytes 1572872 | tf_op jit(solution)/shard_map/ppermute | solution.py:21
  29.1 16.9 %all-to-all-start.1 = ((f32[8,96,64]{1,2,0:T(8,128)}), f32[8,96,64]{1,2,0:T(8,128)S(1)}, u32[]{:S(2)}, u32[]{:S(2)}) async-start(f32[8,96,64]{1,2,0:T(8,128)} %broadcast_in_dim.12), calls=%async_computation.1 | async-start | bytes 524288 | tf_op jit(solution)/shard_map/all_to_all | solution.py:29
  54.2 3.8 %collective-permute-start.3 = (f32[64,16,128]{2,0,1:T(8,128)S(1)}, f32[64,16,128]{2,0,1:T(8,128)S(1)}, u32[]{:S(2)}, u32[]{:S(2)}) collective-permute-start(f32[64,16,128]{2,0,1:T(8,128)S(1)} %bitcast.73), channel_id=1, source_target_pairs={{0,4},{4,0},{1,5},{5,1},{2,6},{6,2},{3,7},{7,3},{8,12},{12,8},{9,1... | collective-permute-start | bytes 1572872 | tf_op jit(solution)/shard_map/ppermute | solution.py:41
  58.2 68.3 %copy-start = (f32[64,128]{1,0:T(8,128)S(1)}, f32[64,128]{1,0:T(8,128)}, u32[]{:S(2)}) copy-start(f32[64,128]{1,0:T(8,128)} %param.2) | copy-start | bytes 98308

commit v2 on v0

v2 whole, which is shorter than its diff:
```python
import functools

import jax
import jax.numpy as jnp
from jax import lax
from jax.experimental import pallas as pl
from jax.experimental.pallas import tpu as pltpu
from jax.sharding import Mesh, PartitionSpec as P

SUB = 8
HI = lax.Precision.HIGHEST
VMEM = pl.BlockSpec(memory_space=pltpu.VMEM)
BIG = pltpu.CompilerParams(vmem_limit_bytes=32 * 2**20)
F32 = jnp.float32


def pack_body(scale, s_ref, o_ref):
    s = s_ref[...]
    k = s.shape[0]
    n = o_ref.shape[0]
    half = k // 2
    gram = lax.dot_general(s, s, (((1,), (1,)), ((), ())), precision=HI, preferred_element_type=F32) * scale
    gram = jnp.concatenate([gram[:half], gram[half:]], axis=1)
    sel = s.T[:SUB]
    sel = jnp.concatenate([sel, jnp.zeros_like(sel)], axis=1)
    o_ref[...] = jnp.broadcast_to(jnp.concatenate([gram, sel], axis=0)[None], o_ref.shape)


def sort_body(x_ref, t_ref, o_ref):
    ng = o_ref.shape[0]
    rows, cols = x_ref.shape
    nx, _, w = t_ref.shape
    k = w // 2
    half = k // 2
    nh = cols // (ng * w)
    gl = ng // 2
    for zl in range(2):
        for j in range(gl):
            for zh in range(nh):
                at = ((zh * 2 + zl) * gl + j) * w
                o_ref[zl * gl + j, zh * rows : (zh + 1) * rows] = x_ref[:, at : at + w]
    sel = [t_ref[x, half:, :k] for x in range(nx)]
    sel = jnp.concatenate([jnp.concatenate(sel[: nx // 2], axis=0), jnp.concatenate(sel[nx // 2 :], axis=0)], axis=1)
    gram = jnp.sum(t_ref[:, :half], axis=0)
    tail = jnp.concatenate([sel, gram], axis=0)
    o_ref[:, nh * rows :] = jnp.broadcast_to(tail[None], (ng, *tail.shape))


def project_body(rows, t_ref, o_ref):
    ng = t_ref.shape[0]
    nh, tall, w = o_ref.shape
    k = w // 2
    at = nh * rows
    sel = [t_ref[g, at : at + rows // 2, h * k : (h + 1) * k] for g in range(ng) for h in range(2)]
    sel = jnp.concatenate(sel, axis=0)
    step = 2
    for z0 in range(0, nh, step):
        wide = [jnp.concatenate([t_ref[g, z * rows : (z + 1) * rows] for g in range(ng)], axis=0) for z in range(z0, z0 + step)]
        res = lax.dot_general(
            sel, jnp.concatenate(wide, axis=1), (((0,), (0,)), ((), ())), precision=HI, preferred_element_type=F32
        )
        for z in range(step):
            o_ref[z0 + z, :k] = res[:, z * w : (z + 1) * w]
    gram = jnp.sum(t_ref[:, at + rows // 2 :], axis=0)
    o_ref[:, k:] = jnp.broadcast_to(gram[None], (nh, tall - k, w))


def finish_body(scale, s_ref, t_ref, q_ref, p_ref):
    k = s_ref.shape[0]
    total = jnp.sum(t_ref[...], axis=0)
    eye = (lax.broadcasted_iota(jnp.int32, (k, k), 0) == lax.broadcasted_iota(jnp.int32, (k, k), 1)).astype(F32)
    gram = jnp.concatenate([total[k:, :k], total[k:, k:]], axis=0)
    m = jnp.concatenate([gram, eye], axis=1)
    row_of = lax.broadcasted_iota(jnp.int32, (k, 1), 0)
    for i in range(k - 1):
        factor = jnp.where(row_of > i, m[:, i : i + 1], 0.0) * (1.0 / m[i : i + 1, i : i + 1])
        m = m - factor * m[i : i + 1, :]
    pivots = jnp.sum(m[:, :k] * eye, axis=1, keepdims=True)
    inv = m[:, k:] * (1.0 / jnp.sqrt(pivots))
    q_ref[...] = jnp.dot(inv, s_ref[...], precision=HI, preferred_element_type=F32)
    p_ref[...] = jnp.dot(inv, total[:k], precision=HI, preferred_element_type=F32) * scale


def call(body, outs, name, *args):
    shapes = [jax.ShapeDtypeStruct(s, F32) for s in outs]
    return pl.pallas_call(
        body, out_shape=shapes, in_specs=[VMEM] * len(args), out_specs=[VMEM] * len(outs), compiler_params=BIG, name=name
    )(*args)


def local(sketch, slab):
    k, sk = sketch.shape
    nh, nl, ny, nc, nx = (lax.axis_size(a) for a in ("zh", "zl", "y", "c", "x"))
    rows, cols = slab.shape
    ng = nl * ny * nc
    out = cols // (nh * ng)
    half = k // 2

    (own,) = call(functools.partial(pack_body, 1.0 / (sk * nh * ng * nx)), [(nx, half + SUB, out)], "pack", sketch)
    own = lax.all_to_all(own, "x", 0, 0, tiled=True)
    (sent,) = call(sort_body, [(ng, nh * rows + rows // 2 + half, out)], "sort", slab, own)
    sent = lax.all_to_all(sent, ("zl", "y", "c"), 0, 0, tiled=True)
    (part,) = call(functools.partial(project_body, rows), [(nh, k + half, out)], "project", sent)
    part = lax.all_to_all(part, "zh", 0, 0, tiled=True)
    scale = 1.0 / (rows * nh * ng) ** 0.5
    ortho, projected = call(functools.partial(finish_body, scale), [(k, sk), (k, out)], "finish", sketch, part)
    return ortho, projected


def solution(mesh):
    nx = mesh.shape["narrow"]
    grid = Mesh(mesh.devices.reshape(-1, 2, 4, 2, nx), ("zh", "zl", "y", "c", "x"))
    wide = ("zh", "zl", "y", "c")
    return jax.shard_map(
        local,
        mesh=grid,
        in_specs=(P(None, (*wide, "x")), P(wide, "x")),
        out_specs=(P(None, (*wide, "x")), P(None, ("x", *wide))),
        check_vma=False,
    )
```

time: 416 us -> 98.5 us (0.24)
  the two profiles are of different devices: /device:TPU:6 before, /device:TPU:8 now
where the time goes in v2:
time: 98.5 us; the launch traced here: 98.2 us
  blocking collectives  87.2 us (89%)
  Pallas kernels  8.01 us (8%)
  local copies, waits for them, and re-layouts  2.35 us (2%)
    all_to_all x1, blocking collectives, local(): part = lax.all_to_all(part, 'zh', 0, 0, tiled=True)  41.8 us
    all_to_all x1, blocking collectives, local(): sent = lax.all_to_all(sent, ('zl', 'y', 'c'), 0, 0, tiled=True)  35.6 us
    all_to_all x1, blocking collectives, local(): own = lax.all_to_all(own, 'x', 0, 0, tiled=True)  9.82 us
    pallas_call x4, Pallas kernels, call(): pl.pallas_call(body, out_shape=shapes, in_specs=[VMEM] * len(args), out_s...  8.01 us
    unnamed x6, local copies, waits for them, and re-layouts  2.35 us

profile of v2, /device:TPU:8, one launch (start us, length us, event | category | flops | bytes accessed | tf_op | source)
XLA Modules:
  0.0 98.2 jit_solution(15290921697073069433)
XLA Ops:
  0.6 0.0 copy-start.1
  0.6 0.7 copy-done.1
  1.4 0.2 pack.1
  1.6 9.8 %all_to_all.15.t_ref = f32[4,40,128]{2,1,0:T(8,128)S(1)} all-to-all(f32[4,40,128]{2,1,0:T(8,128)S(1)} %pack.1), channel_id=1, replica_groups=mesh['zh'=8,'zl'=2,'y'=4,'c'=2,'x'=4] {'x'}, dimensions={0} | all-to-all | bytes 163840 | tf_op jit(solution)/shard_map/all_to_all | solution.py:100
  11.5 0.0 copy-start
  11.5 1.6 %copy-done = f32[32,16384]{1,0:T(8,128)S(1)} copy-done((f32[32,16384]{1,0:T(8,128)S(1)}, f32[32,16384]{1,0:T(8,128)}, u32[]{:S(2)}) %copy-start) | copy-done | bytes 2097176
  13.0 0.2 sort.1
  13.2 35.6 %all_to_all.16.t_ref = f32[16,304,128]{2,1,0:T(8,128)S(1)} all-to-all(f32[16,304,128]{2,1,0:T(8,128)S(1)} %sort.1), channel_id=1, replica_groups=mesh['zh'=8,'zl'=2,'y'=4,'c'=2,'x'=4] {'zl','y','c'}, dimensions={0} | all-to-all | bytes 4980736 | tf_op jit(solution)/shard_map/all_to_all | solution.py:102
  48.8 0.0 copy-start.2
  48.8 1.4 %project.1 = f32[8,96,128]{2,1,0:T(8,128)S(1)} custom-call(f32[16,304,128]{2,1,0:T(8,128)S(1)} %all_to_all.16.t_ref), custom_call_target="tpu_custom_call" | custom-call | tf_op jit(solution)/shard_map/project/pallas_call | solution.py:86
  50.2 41.8 %all_to_all.17.t_ref = f32[8,96,128]{2,1,0:T(8,128)S(1)} all-to-all(f32[8,96,128]{2,1,0:T(8,128)S(1)} %project.1), channel_id=1, replica_groups=mesh['zh'=8,'zl'=2,'y'=4,'c'=2,'x'=4] {'zh'}, dimensions={0} | all-to-all | bytes 786432 | tf_op jit(solution)/shard_map/all_to_all | solution.py:104
  92.0 0.0 copy-done.2
  92.0 6.2 %finish.1 = (f32[64,128]{1,0:T(8,128)}, f32[64,128]{1,0:T(8,128)}) custom-call(f32[64,128]{1,0:T(8,128)S(1)} %copy-done.2, f32[8,96,128]{2,1,0:T(8,128)S(1)} %all_to_all.17.t_ref), custom_call_target="tpu_custom_call" | custom-call | tf_op jit(solution)/shard_map/finish/pallas_call | solution.py:86
Async XLA Ops:
  0.6 0.8 copy-start.1
  11.5 1.6 %copy-start = (f32[32,16384]{1,0:T(8,128)S(1)}, f32[32,16384]{1,0:T(8,128)}, u32[]{:S(2)}) copy-start(f32[32,16384]{1,0:T(8,128)} %x_ref.1) | copy-start | bytes 6291460
  48.8 43.2 %copy-start.2 = (f32[64,128]{1,0:T(8,128)S(1)}, f32[64,128]{1,0:T(8,128)}, u32[]{:S(2)}) copy-start(f32[64,128]{1,0:T(8,128)} %s_ref.3) | copy-start | bytes 98308

commit v3 on v2

v3 whole, which is shorter than its diff:
```python
import functools

import jax
import jax.numpy as jnp
from jax import lax
from jax.experimental import pallas as pl
from jax.experimental.pallas import tpu as pltpu
from jax.sharding import Mesh, PartitionSpec as P

SUB = 8
HI = lax.Precision.HIGHEST
SMEM = pl.BlockSpec(memory_space=pltpu.SMEM)
VMEM = pl.BlockSpec(memory_space=pltpu.VMEM)
BIG = pltpu.CompilerParams(vmem_limit_bytes=32 * 2**20)
F32 = jnp.float32


def pack_body(scale, s_ref, o_ref):
    s = s_ref[...]
    k = s.shape[0]
    half = k // 2
    gram = lax.dot_general(s, s, (((1,), (1,)), ((), ())), precision=HI, preferred_element_type=F32) * scale
    gram = jnp.concatenate([gram[:half], gram[half:]], axis=1)
    sel = s.T[:SUB]
    sel = jnp.concatenate([sel, jnp.zeros_like(sel)], axis=1)
    o_ref[...] = jnp.broadcast_to(jnp.concatenate([gram, sel], axis=0)[None], o_ref.shape)


def away_body(w, at_ref, x_ref, o_ref):
    for b in range(o_ref.shape[1] // w):
        col = pl.multiple_of((2 * b + 1 - at_ref[0]) * w, w)
        o_ref[:, b * w : (b + 1) * w] = x_ref[:, pl.ds(col, w)]


def sort_body(ny, at_ref, x_ref, a_ref, t_ref, o_ref):
    ng = o_ref.shape[0]
    rows = x_ref.shape[0]
    _, tall, w = t_ref.shape
    nh = a_ref.shape[1] // (ng * w)
    k = w // 2
    half = k // 2
    c = at_ref[0]
    mine = pl.multiple_of(c * rows, rows)
    other = pl.multiple_of((1 - c) * rows, rows)
    for g in range(ng):
        for zh in range(nh):
            b = (zh * 2 + g // ny) * ny + g % ny
            base = zh * 2 * rows
            o_ref[g, pl.ds(base + mine, rows)] = x_ref[:, pl.ds(pl.multiple_of((2 * b + c) * w, w), w)]
            o_ref[g, pl.ds(base + other, rows)] = a_ref[:, b * w : (b + 1) * w]
    n = t_ref.shape[0]
    sel = [t_ref[p, half:, :k] for p in range(n)]
    sel = jnp.concatenate([jnp.concatenate(sel[: n // 2], axis=0), jnp.concatenate(sel[n // 2 :], axis=0)], axis=1)
    gram = jnp.sum(t_ref[:, :half], axis=0)
    tail = jnp.concatenate([sel, gram], axis=0)
    o_ref[:, nh * 2 * rows :] = jnp.broadcast_to(tail[None], (ng, *tail.shape))


def project_body(rows, t_ref, o_ref):
    ng = t_ref.shape[0]
    nh, tall, w = o_ref.shape
    k = w // 2
    at = nh * rows
    sel = [t_ref[g, at : at + rows // 2, h * k : (h + 1) * k] for g in range(ng) for h in range(2)]
    sel = jnp.concatenate(sel, axis=0)
    step = 2
    for z0 in range(0, nh, step):
        wide = [jnp.concatenate([t_ref[g, z * rows : (z + 1) * rows] for g in range(ng)], axis=0) for z in range(z0, z0 + step)]
        res = lax.dot_general(
            sel, jnp.concatenate(wide, axis=1), (((0,), (0,)), ((), ())), precision=HI, preferred_element_type=F32
        )
        for z in range(step):
            o_ref[z0 + z, :k] = res[:, z * w : (z + 1) * w]
    gram = jnp.sum(t_ref[:, at + rows // 2 :], axis=0)
    o_ref[:, k:] = jnp.broadcast_to(gram[None], (nh, tall - k, w))


def inverse_factor(gram):
    k = gram.shape[0]
    eye = (lax.broadcasted_iota(jnp.int32, (k, k), 0) == lax.broadcasted_iota(jnp.int32, (k, k), 1)).astype(F32)
    m = jnp.concatenate([gram, eye], axis=1).reshape(k // SUB, SUB, 2 * k)
    tile = (SUB, 2 * k)
    row_of = lax.broadcasted_iota(jnp.int32, m.shape, 0) * SUB + lax.broadcasted_iota(jnp.int32, m.shape, 1)
    step = 4
    for i in range(0, k, step):
        js = range(step)
        rows = [jnp.broadcast_to(m[(i + j) // SUB, (i + j) % SUB : (i + j) % SUB + 1], tile) for j in js]
        cols = [jnp.broadcast_to(m[:, :, i + j : i + j + 1], m.shape) for j in js]
        piv = [[jnp.broadcast_to(rows[j][:, i + q : i + q + 1], tile) if q >= j else None for q in js] for j in js]
        for j in js:
            inv = 1.0 / piv[j][j]
            for q in range(j + 1, step):
                f = piv[j][q] * inv
                rows[q] = rows[q] - f * rows[j]
                cols[q] = cols[q] - f[None] * cols[j]
                for r in range(q, step):
                    piv[q][r] = piv[q][r] - f * piv[j][r]
            m = m - jnp.where(row_of > i + j, cols[j], 0.0) * (inv * rows[j])[None]
    m = m.reshape(k, 2 * k)
    pivots = jnp.sum(m[:, :k] * eye, axis=1, keepdims=True)
    return m[:, k:] * (1.0 / jnp.sqrt(pivots))


def finish_body(scale, s_ref, t_ref, q_ref, p_ref):
    k, sk = s_ref.shape
    total = jnp.sum(t_ref[...], axis=0)
    inv = inverse_factor(jnp.concatenate([total[k:, :k], total[k:, k:]], axis=0))
    both = jnp.concatenate([s_ref[...], total[:k] * scale], axis=1)
    both = jnp.dot(inv, both, precision=HI, preferred_element_type=F32)
    q_ref[...] = both[:, :sk]
    p_ref[...] = both[:, sk:]


def call(body, outs, name, *args):
    shapes = [jax.ShapeDtypeStruct(s, F32) for s in outs]
    where = [SMEM if a.ndim == 1 else VMEM for a in args]
    return pl.pallas_call(
        body, out_shape=shapes, in_specs=where, out_specs=[VMEM] * len(outs), compiler_params=BIG, name=name
    )(*args)


def local(sketch, slab):
    k, sk = sketch.shape
    nh, nl, ny, nc, nx = (lax.axis_size(a) for a in ("zh", "zl", "y", "c", "x"))
    rows, cols = slab.shape
    ng = nl * ny
    out = cols // (nh * ng * nc)
    half = k // 2
    at = lax.axis_index("c").astype(jnp.int32)[None]

    (own,) = call(functools.partial(pack_body, 1.0 / (sk * nh * ng * nc * nx)), [(nc * nx, half + SUB, out)], "pack", sketch)
    own = lax.all_to_all(own, ("c", "x"), 0, 0, tiled=True)
    (away,) = call(functools.partial(away_body, out), [(rows, cols // nc)], "away", at, slab)
    away = lax.ppermute(away, "c", [(0, 1), (1, 0)])
    rows *= nc
    (sent,) = call(functools.partial(sort_body, ny), [(ng, nh * rows + rows // 2 + half, out)], "sort", at, slab, away, own)
    sent = lax.all_to_all(sent, ("zl", "y"), 0, 0, tiled=True)
    (part,) = call(functools.partial(project_body, rows), [(nh, k + half, out)], "project", sent)
    part = lax.all_to_all(part, "zh", 0, 0, tiled=True)
    scale = 1.0 / (rows * nh * ng) ** 0.5
    ortho, projected = call(functools.partial(finish_body, scale), [(k, sk), (k, out)], "finish", sketch, part)
    return ortho, projected


def solution(mesh):
    nx = mesh.shape["narrow"]
    grid = Mesh(mesh.devices.reshape(-1, 2, 4, 2, nx), ("zh", "zl", "y", "c", "x"))
    wide = ("zh", "zl", "y", "c")
    return jax.shard_map(
        local,
        mesh=grid,
        in_specs=(P(None, (*wide, "x")), P(wide, "x")),
        out_specs=(P(None, (*wide, "x")), P(None, ("x", *wide))),
        check_vma=False,
    )
```

time: 98.5 us -> 94.7 us (0.961)
  the two profiles are of different devices: /device:TPU:8 before, /device:TPU:6 now
where the time goes in v3:
time: 94.7 us; the launch traced here: 92.9 us
  blocking collectives  82.8 us (87%)
  Pallas kernels  5.72 us (6%)
  starting transfers between devices  2.05 us (2%)
  local copies, waits for them, and re-layouts  1.59 us (2%)
    all_to_all x1, blocking collectives, local(): part = lax.all_to_all(part, 'zh', 0, 0, tiled=True)  37.7 us
    all_to_all x1, blocking collectives, local(): sent = lax.all_to_all(sent, ('zl', 'y'), 0, 0, tiled=True)  32.5 us
    all_to_all x1, blocking collectives, local(): own = lax.all_to_all(own, ('c', 'x'), 0, 0, tiled=True)  12.7 us
    pallas_call x5, Pallas kernels, call(): pl.pallas_call(body, out_shape=shapes, in_specs=where, out_specs=[VMEM] *...  5.72 us
    ppermute x1, starting transfers between devices, local(): away = lax.ppermute(away, 'c', [(0, 1), (1, 0)])  2.05 us
  transfers between devices with their start and end apart: 1, of which 0 were waited for; matrix products, arithmetic and copies ran while one was open for 0% of the time, Pallas kernels for 0%

profile of v3, /device:TPU:6, one launch (start us, length us, event | category | flops | bytes accessed | tf_op | source)
XLA Modules:
  0.0 92.9 jit_solution(2766673410480052021)
XLA Ops:
  0.6 0.0 copy-start
  0.6 1.6 %copy-done = f32[32,16384]{1,0:T(8,128)S(1)} copy-done((f32[32,16384]{1,0:T(8,128)S(1)}, f32[32,16384]{1,0:T(8,128)}, u32[]{:S(2)}) %copy-start) | copy-done | bytes 2097176
  2.2 0.0 copy-start.2
  2.2 0.0 copy-start.1
  2.2 0.1 away.1
  2.4 2.1 %collective-permute-start = (f32[32,8192]{1,0:T(8,128)S(1)}, f32[32,8192]{1,0:T(8,128)S(1)}, u32[]{:S(2)}, u32[]{:S(2)}) collective-permute-start(f32[32,8192]{1,0:T(8,128)S(1)} %away.1), channel_id=1, source_target_pairs={{0,4},{4,0},{1,5},{5,1},{2,6},{6,2},{3,7},{7,3},{8,12},{12,8},{9,1... | collective-permute-start | bytes 3145736 | tf_op jit(solution)/shard_map/ppermute | solution.py:134
  4.4 0.0 copy-done.2
  4.4 0.3 pack.1
  4.7 12.7 %all_to_all.15.t_ref = f32[8,40,128]{2,1,0:T(8,128)S(1)} all-to-all(f32[8,40,128]{2,1,0:T(8,128)S(1)} %pack.1), channel_id=1, replica_groups=mesh['zh'=8,'zl'=2,'y'=4,'c'=2,'x'=4] {'c','x'}, dimensions={0} | all-to-all | bytes 327680 | tf_op jit(solution)/shard_map/all_to_all | solution.py:132
  17.4 0.0 collective-permute-done.a_ref
  17.4 0.0 copy-done.1
  17.4 0.2 sort.1
  17.6 32.5 %all_to_all.16.t_ref = f32[8,576,128]{2,1,0:T(8,128)S(1)} all-to-all(f32[8,576,128]{2,1,0:T(8,128)S(1)} %sort.1), channel_id=1, replica_groups=mesh['zh'=8,'zl'=2,'y'=4,'c'=2,'x'=4] {'zl','y'}, dimensions={0} | all-to-all | bytes 4718592 | tf_op jit(solution)/shard_map/all_to_all | solution.py:137
  50.1 1.4 %project.1 = f32[8,96,128]{2,1,0:T(8,128)S(1)} custom-call(f32[8,576,128]{2,1,0:T(8,128)S(1)} %all_to_all.16.t_ref), custom_call_target="tpu_custom_call" | custom-call | tf_op jit(solution)/shard_map/project/pallas_call | solution.py:117
  51.5 37.7 %all_to_all.17.t_ref = f32[8,96,128]{2,1,0:T(8,128)S(1)} all-to-all(f32[8,96,128]{2,1,0:T(8,128)S(1)} %project.1), channel_id=1, replica_groups=mesh['zh'=8,'zl'=2,'y'=4,'c'=2,'x'=4] {'zh'}, dimensions={0} | all-to-all | bytes 786432 | tf_op jit(solution)/shard_map/all_to_all | solution.py:139
  89.1 3.7 %finish.1 = (f32[64,128]{1,0:T(8,128)}, f32[64,128]{1,0:T(8,128)}) custom-call(f32[64,128]{1,0:T(8,128)S(1)} %copy-done.2, f32[8,96,128]{2,1,0:T(8,128)S(1)} %all_to_all.17.t_ref), custom_call_target="tpu_custom_call" | custom-call | tf_op jit(solution)/shard_map/finish/pallas_call | solution.py:117
Async XLA Ops:
  0.6 1.6 %copy-start = (f32[32,16384]{1,0:T(8,128)S(1)}, f32[32,16384]{1,0:T(8,128)}, u32[]{:S(2)}) copy-start(f32[32,16384]{1,0:T(8,128)} %x_ref.3) | copy-start | bytes 6291460
  2.2 2.2 %copy-start.2 = (f32[64,128]{1,0:T(8,128)S(1)}, f32[64,128]{1,0:T(8,128)}, u32[]{:S(2)}) copy-start(f32[64,128]{1,0:T(8,128)} %s_ref.3) | copy-start | bytes 98308
  2.2 15.1 %copy-start.1 = (f32[32,16384]{1,0:T(8,128)S(1)}, f32[32,16384]{1,0:T(8,128)}, u32[]{:S(2)}) copy-start(f32[32,16384]{1,0:T(8,128)} %x_ref.3) | copy-start | bytes 6291460
  2.4 15.0 %collective-permute-start = (f32[32,8192]{1,0:T(8,128)S(1)}, f32[32,8192]{1,0:T(8,128)S(1)}, u32[]{:S(2)}, u32[]{:S(2)}) collective-permute-start(f32[32,8192]{1,0:T(8,128)S(1)} %away.1), channel_id=1, source_target_pairs={{0,4},{4,0},{1,5},{5,1},{2,6},{6,2},{3,7},{7,3},{8,12},{12,8},{9,1... | collective-permute-start | bytes 3145736 | tf_op jit(solution)/shard_map/ppermute | solution.py:134

commit v4 on v3

--- a/solution.py
+++ b/solution.py
@@ -15,15 +15,42 @@
 F32 = jnp.float32
 
 
+GRAM = 24
+
+
+def fold(gram):
+    k = gram.shape[0]
+    h, q = k // 2, k // 4
+    a, b, c = gram[:h, :h], gram[:h, h:], gram[h:, h:]
+    row, col = (lax.broadcasted_iota(jnp.int32, (h, h), d) for d in (0, 1))
+    both = jnp.concatenate([jnp.where(row > col, a, c), b], axis=1)
+    both = jnp.concatenate([both[:q], both[q:]], axis=1)
+    diag = jnp.sum(jnp.where(row == col, a, 0.0), axis=0, keepdims=True)
+    diag = jnp.concatenate([diag, jnp.zeros((1, 2 * k - h), F32)], axis=1)
+    return jnp.concatenate([both, diag, jnp.zeros((GRAM - q - 1, 2 * k), F32)], axis=0)
+
+
+def unfold(tile):
+    k = tile.shape[1] // 2
+    h, q = k // 2, k // 4
+    both = jnp.concatenate([tile[:q, :k], tile[:q, k:]], axis=0)
+    turned = both.T
+    row, col = (lax.broadcasted_iota(jnp.int32, (h, h), d) for d in (0, 1))
+    x, xt = both[:, :h], turned[:h]
+    diag = jnp.broadcast_to(tile[q : q + 1, :h], (h, h))
+    a = jnp.where(row > col, x, jnp.where(row < col, xt, diag))
+    c = jnp.where(row <= col, x, xt)
+    return jnp.concatenate(
+        [jnp.concatenate([a, both[:, h:]], axis=1), jnp.concatenate([turned[h:], c], axis=1)], axis=0
+    )
+
+
 def pack_body(scale, s_ref, o_ref):
     s = s_ref[...]
-    k = s.shape[0]
-    half = k // 2
     gram = lax.dot_general(s, s, (((1,), (1,)), ((), ())), precision=HI, preferred_element_type=F32) * scale
-    gram = jnp.concatenate([gram[:half], gram[half:]], axis=1)
     sel = s.T[:SUB]
     sel = jnp.concatenate([sel, jnp.zeros_like(sel)], axis=1)
-    o_ref[...] = jnp.broadcast_to(jnp.concatenate([gram, sel], axis=0)[None], o_ref.shape)
+    o_ref[...] = jnp.broadcast_to(jnp.concatenate([fold(gram), sel], axis=0)[None], o_ref.shape)
 
 
 def away_body(w, at_ref, x_ref, o_ref):
@@ -38,7 +65,7 @@
     _, tall, w = t_ref.shape
     nh = a_ref.shape[1] // (ng * w)
     k = w // 2
-    half = k // 2
+    half = tall - SUB
     c = at_ref[0]
     mine = pl.multiple_of(c * rows, rows)
     other = pl.multiple_of((1 - c) * rows, rows)
@@ -81,7 +108,7 @@
     m = jnp.concatenate([gram, eye], axis=1).reshape(k // SUB, SUB, 2 * k)
     tile = (SUB, 2 * k)
     row_of = lax.broadcasted_iota(jnp.int32, m.shape, 0) * SUB + lax.broadcasted_iota(jnp.int32, m.shape, 1)
-    step = 4
+    step = SUB
     for i in range(0, k, step):
         js = range(step)
         rows = [jnp.broadcast_to(m[(i + j) // SUB, (i + j) % SUB : (i + j) % SUB + 1], tile) for j in js]
@@ -104,7 +131,7 @@
 def finish_body(scale, s_ref, t_ref, q_ref, p_ref):
     k, sk = s_ref.shape
     total = jnp.sum(t_ref[...], axis=0)
-    inv = inverse_factor(jnp.concatenate([total[k:, :k], total[k:, k:]], axis=0))
+    inv = inverse_factor(unfold(total[k:]))
     both = jnp.concatenate([s_ref[...], total[:k] * scale], axis=1)
     both = jnp.dot(inv, both, precision=HI, preferred_element_type=F32)
     q_ref[...] = both[:, :sk]
@@ -125,17 +152,16 @@
     rows, cols = slab.shape
     ng = nl * ny
     out = cols // (nh * ng * nc)
-    half = k // 2
     at = lax.axis_index("c").astype(jnp.int32)[None]
 
-    (own,) = call(functools.partial(pack_body, 1.0 / (sk * nh * ng * nc * nx)), [(nc * nx, half + SUB, out)], "pack", sketch)
+    (own,) = call(functools.partial(pack_body, 1.0 / (sk * nh * ng * nc * nx)), [(nc * nx, GRAM + SUB, out)], "pack", sketch)
     own = lax.all_to_all(own, ("c", "x"), 0, 0, tiled=True)
     (away,) = call(functools.partial(away_body, out), [(rows, cols // nc)], "away", at, slab)
     away = lax.ppermute(away, "c", [(0, 1), (1, 0)])
     rows *= nc
-    (sent,) = call(functools.partial(sort_body, ny), [(ng, nh * rows + rows // 2 + half, out)], "sort", at, slab, away, own)
+    (sent,) = call(functools.partial(sort_body, ny), [(ng, nh * rows + rows // 2 + GRAM, out)], "sort", at, slab, away, own)
     sent = lax.all_to_all(sent, ("zl", "y"), 0, 0, tiled=True)
-    (part,) = call(functools.partial(project_body, rows), [(nh, k + half, out)], "project", sent)
+    (part,) = call(functools.partial(project_body, rows), [(nh, k + GRAM, out)], "project", sent)
     part = lax.all_to_all(part, "zh", 0, 0, tiled=True)
     scale = 1.0 / (rows * nh * ng) ** 0.5
     ortho, projected = call(functools.partial(finish_body, scale), [(k, sk), (k, out)], "finish", sketch, part)

time: 94.7 us -> 92.5 us (0.977)
  the two profiles are of different devices: /device:TPU:6 before, /device:TPU:2 now
where the time goes in v4:
time: 92.5 us; the launch traced here: 92.2 us
  blocking collectives  82.8 us (90%)
  Pallas kernels  5.07 us (5%)
  starting transfers between devices  2.05 us (2%)
  local copies, waits for them, and re-layouts  1.59 us (2%)
    all_to_all x1, blocking collectives, local(): part = lax.all_to_all(part, 'zh', 0, 0, tiled=True)  37.7 us
    all_to_all x1, blocking collectives, local(): sent = lax.all_to_all(sent, ('zl', 'y'), 0, 0, tiled=True)  32.3 us
    all_to_all x1, blocking collectives, local(): own = lax.all_to_all(own, ('c', 'x'), 0, 0, tiled=True)  12.8 us
    pallas_call x5, Pallas kernels, call(): pl.pallas_call(body, out_shape=shapes, in_specs=where, out_specs=[VMEM] *...  5.07 us
    ppermute x1, starting transfers between devices, local(): away = lax.ppermute(away, 'c', [(0, 1), (1, 0)])  2.05 us
  transfers between devices with their start and end apart: 1, of which 0 were waited for; matrix products, arithmetic and copies ran while one was open for 0% of the time, Pallas kernels for 0%

profile of v4, /device:TPU:2, one launch (start us, length us, event | category | flops | bytes accessed | tf_op | source)
XLA Modules:
  0.0 92.2 jit_solution(5407167276201584510)
XLA Ops:
  0.6 0.0 copy-start
  0.6 1.6 %copy-done = f32[32,16384]{1,0:T(8,128)S(1)} copy-done((f32[32,16384]{1,0:T(8,128)S(1)}, f32[32,16384]{1,0:T(8,128)}, u32[]{:S(2)}) %copy-start) | copy-done | bytes 2097176
  2.2 0.0 copy-start.2
  2.2 0.0 copy-start.1
  2.2 0.1 away.1
  2.4 2.1 %collective-permute-start = (f32[32,8192]{1,0:T(8,128)S(1)}, f32[32,8192]{1,0:T(8,128)S(1)}, u32[]{:S(2)}, u32[]{:S(2)}) collective-permute-start(f32[32,8192]{1,0:T(8,128)S(1)} %away.1), channel_id=1, source_target_pairs={{0,4},{4,0},{1,5},{5,1},{2,6},{6,2},{3,7},{7,3},{8,12},{12,8},{9,1... | collective-permute-start | bytes 3145736 | tf_op jit(solution)/shard_map/ppermute | solution.py:160
  4.4 0.0 copy-done.2
  4.4 0.3 pack.1
  4.7 12.8 %all_to_all.15.t_ref = f32[8,32,128]{2,1,0:T(8,128)S(1)} all-to-all(f32[8,32,128]{2,1,0:T(8,128)S(1)} %pack.1), channel_id=1, replica_groups=mesh['zh'=8,'zl'=2,'y'=4,'c'=2,'x'=4] {'c','x'}, dimensions={0} | all-to-all | bytes 262144 | tf_op jit(solution)/shard_map/all_to_all | solution.py:158
  17.6 0.0 collective-permute-done.a_ref
  17.6 0.0 copy-done.1
  17.6 0.2 sort.1
  17.8 32.3 %all_to_all.16.t_ref = f32[8,568,128]{2,1,0:T(8,128)S(1)} all-to-all(f32[8,568,128]{2,1,0:T(8,128)S(1)} %sort.1), channel_id=1, replica_groups=mesh['zh'=8,'zl'=2,'y'=4,'c'=2,'x'=4] {'zl','y'}, dimensions={0} | all-to-all | bytes 4653056 | tf_op jit(solution)/shard_map/all_to_all | solution.py:163
  50.1 1.4 %project.1 = f32[8,88,128]{2,1,0:T(8,128)S(1)} custom-call(f32[8,568,128]{2,1,0:T(8,128)S(1)} %all_to_all.16.t_ref), custom_call_target="tpu_custom_call" | custom-call | tf_op jit(solution)/shard_map/project/pallas_call | solution.py:144
  51.5 37.7 %all_to_all.17.t_ref = f32[8,88,128]{2,1,0:T(8,128)S(1)} all-to-all(f32[8,88,128]{2,1,0:T(8,128)S(1)} %project.1), channel_id=1, replica_groups=mesh['zh'=8,'zl'=2,'y'=4,'c'=2,'x'=4] {'zh'}, dimensions={0} | all-to-all | bytes 720896 | tf_op jit(solution)/shard_map/all_to_all | solution.py:165
  89.2 3.1 %finish.1 = (f32[64,128]{1,0:T(8,128)}, f32[64,128]{1,0:T(8,128)}) custom-call(f32[64,128]{1,0:T(8,128)S(1)} %copy-done.2, f32[8,88,128]{2,1,0:T(8,128)S(1)} %all_to_all.17.t_ref), custom_call_target="tpu_custom_call" | custom-call | tf_op jit(solution)/shard_map/finish/pallas_call | solution.py:144
Async XLA Ops:
  0.6 1.6 %copy-start = (f32[32,16384]{1,0:T(8,128)S(1)}, f32[32,16384]{1,0:T(8,128)}, u32[]{:S(2)}) copy-start(f32[32,16384]{1,0:T(8,128)} %x_ref.3) | copy-start | bytes 6291460
  2.2 2.2 %copy-start.2 = (f32[64,128]{1,0:T(8,128)S(1)}, f32[64,128]{1,0:T(8,128)}, u32[]{:S(2)}) copy-start(f32[64,128]{1,0:T(8,128)} %s_ref.3) | copy-start | bytes 98308
  2.2 15.3 %copy-start.1 = (f32[32,16384]{1,0:T(8,128)S(1)}, f32[32,16384]{1,0:T(8,128)}, u32[]{:S(2)}) copy-start(f32[32,16384]{1,0:T(8,128)} %x_ref.3) | copy-start | bytes 6291460
  2.4 15.2 %collective-permute-start = (f32[32,8192]{1,0:T(8,128)S(1)}, f32[32,8192]{1,0:T(8,128)S(1)}, u32[]{:S(2)}, u32[]{:S(2)}) collective-permute-start(f32[32,8192]{1,0:T(8,128)S(1)} %away.1), channel_id=1, source_target_pairs={{0,4},{4,0},{1,5},{5,1},{2,6},{6,2},{3,7},{7,3},{8,12},{12,8},{9,1... | collective-permute-start | bytes 3145736 | tf_op jit(solution)/shard_map/ppermute | solution.py:160

commit v5 on v4

--- a/solution.py
+++ b/solution.py
@@ -13,6 +13,7 @@
 VMEM = pl.BlockSpec(memory_space=pltpu.VMEM)
 BIG = pltpu.CompilerParams(vmem_limit_bytes=32 * 2**20)
 F32 = jnp.float32
+PLACE = (0, 4, 2, 6, 1, 5, 3, 7)
 
 
 GRAM = 24
@@ -97,7 +98,7 @@
             sel, jnp.concatenate(wide, axis=1), (((0,), (0,)), ((), ())), precision=HI, preferred_element_type=F32
         )
         for z in range(step):
-            o_ref[z0 + z, :k] = res[:, z * w : (z + 1) * w]
+            o_ref[PLACE[z0 + z], :k] = res[:, z * w : (z + 1) * w]
     gram = jnp.sum(t_ref[:, at + rows // 2 :], axis=0)
     o_ref[:, k:] = jnp.broadcast_to(gram[None], (nh, tall - k, w))
 
@@ -148,7 +149,8 @@
 
 def local(sketch, slab):
     k, sk = sketch.shape
-    nh, nl, ny, nc, nx = (lax.axis_size(a) for a in ("zh", "zl", "y", "c", "x"))
+    nl, ny, nc, nx = (lax.axis_size(a) for a in ("zl", "y", "c", "x"))
+    nh = len(PLACE)
     rows, cols = slab.shape
     ng = nl * ny
     out = cols // (nh * ng * nc)
@@ -162,7 +164,7 @@
     (sent,) = call(functools.partial(sort_body, ny), [(ng, nh * rows + rows // 2 + GRAM, out)], "sort", at, slab, away, own)
     sent = lax.all_to_all(sent, ("zl", "y"), 0, 0, tiled=True)
     (part,) = call(functools.partial(project_body, rows), [(nh, k + GRAM, out)], "project", sent)
-    part = lax.all_to_all(part, "zh", 0, 0, tiled=True)
+    part = lax.all_to_all(part, ("z2", "z1", "z0"), 0, 0, tiled=True)
     scale = 1.0 / (rows * nh * ng) ** 0.5
     ortho, projected = call(functools.partial(finish_body, scale), [(k, sk), (k, out)], "finish", sketch, part)
     return ortho, projected
@@ -170,8 +172,8 @@
 
 def solution(mesh):
     nx = mesh.shape["narrow"]
-    grid = Mesh(mesh.devices.reshape(-1, 2, 4, 2, nx), ("zh", "zl", "y", "c", "x"))
-    wide = ("zh", "zl", "y", "c")
+    grid = Mesh(mesh.devices.reshape(2, 2, 2, 2, 4, 2, nx), ("z0", "z1", "z2", "zl", "y", "c", "x"))
+    wide = ("z0", "z1", "z2", "zl", "y", "c")
     return jax.shard_map(
         local,
         mesh=grid,

time: 92.5 us -> 90.4 us (0.977)
  the two profiles are of different devices: /device:TPU:2 before, /device:TPU:32 now
where the time goes in v5:
time: 90.4 us; the launch traced here: 90.1 us
  blocking collectives  80.7 us (89%)
  Pallas kernels  5.07 us (6%)
  starting transfers between devices  2.05 us (2%)
  local copies, waits for them, and re-layouts  1.59 us (2%)
    all_to_all x1, blocking collectives, local(): part = lax.all_to_all(part, ('z2', 'z1', 'z0'), 0, 0, tiled=True)  36.4 us
    all_to_all x1, blocking collectives, local(): sent = lax.all_to_all(sent, ('zl', 'y'), 0, 0, tiled=True)  34.6 us
    all_to_all x1, blocking collectives, local(): own = lax.all_to_all(own, ('c', 'x'), 0, 0, tiled=True)  9.78 us
    pallas_call x5, Pallas kernels, call(): pl.pallas_call(body, out_shape=shapes, in_specs=where, out_specs=[VMEM] *...  5.07 us
    ppermute x1, starting transfers between devices, local(): away = lax.ppermute(away, 'c', [(0, 1), (1, 0)])  2.05 us
  transfers between devices with their start and end apart: 1, of which 0 were waited for; matrix products, arithmetic and copies ran while one was open for 0% of the time, Pallas kernels for 0%

profile of v5, /device:TPU:32, one launch (start us, length us, event | category | flops | bytes accessed | tf_op | source)
XLA Modules:
  0.0 90.1 jit_solution(688520085496243137)
XLA Ops:
  0.6 0.0 copy-start
  0.6 1.6 %copy-done = f32[32,16384]{1,0:T(8,128)S(1)} copy-done((f32[32,16384]{1,0:T(8,128)S(1)}, f32[32,16384]{1,0:T(8,128)}, u32[]{:S(2)}) %copy-start) | copy-done | bytes 2097176
  2.2 0.0 copy-start.2
  2.2 0.0 copy-start.1
  2.2 0.1 away.1
  2.4 2.1 %collective-permute-start = (f32[32,8192]{1,0:T(8,128)S(1)}, f32[32,8192]{1,0:T(8,128)S(1)}, u32[]{:S(2)}, u32[]{:S(2)}) collective-permute-start(f32[32,8192]{1,0:T(8,128)S(1)} %away.1), channel_id=1, source_target_pairs={{0,4},{4,0},{1,5},{5,1},{2,6},{6,2},{3,7},{7,3},{8,12},{12,8},{9,1... | collective-permute-start | bytes 3145736 | tf_op jit(solution)/shard_map/ppermute | solution.py:162
  4.4 0.0 copy-done.2
  4.4 0.3 pack.1
  4.7 9.8 %all_to_all.15.t_ref = f32[8,32,128]{2,1,0:T(8,128)S(1)} all-to-all(f32[8,32,128]{2,1,0:T(8,128)S(1)} %pack.1), channel_id=1, replica_groups=mesh['z0'=2,'z1'=2,'z2'=2,'zl'=2,'y'=4,'c'=2,'x'=4] {'c','x'}, dimensions={0} | all-to-all | bytes 262144 | tf_op jit(solution)/shard_map/all_to_all | solution.py:160
  14.5 0.0 collective-permute-done.a_ref
  14.5 0.0 copy-done.1
  14.5 0.2 sort.1
  14.8 34.6 %all_to_all.16.t_ref = f32[8,568,128]{2,1,0:T(8,128)S(1)} all-to-all(f32[8,568,128]{2,1,0:T(8,128)S(1)} %sort.1), channel_id=1, replica_groups=mesh['z0'=2,'z1'=2,'z2'=2,'zl'=2,'y'=4,'c'=2,'x'=4] {'zl','y'}, dimensions={0} | all-to-all | bytes 4653056 | tf_op jit(solution)/shard_map/all_to_all | solution.py:165
  49.3 1.4 %project.1 = f32[8,88,128]{2,1,0:T(8,128)S(1)} custom-call(f32[8,568,128]{2,1,0:T(8,128)S(1)} %all_to_all.16.t_ref), custom_call_target="tpu_custom_call" | custom-call | tf_op jit(solution)/shard_map/project/pallas_call | solution.py:145
  50.7 36.4 %all_to_all.17.t_ref = f32[8,88,128]{2,1,0:T(8,128)S(1)} all-to-all(f32[8,88,128]{2,1,0:T(8,128)S(1)} %project.1), channel_id=1, replica_groups=mesh['z0'=2,'z1'=2,'z2'=2,'zl'=2,'y'=4,'c'=2,'x'=4] {'z2','z1','z0'}, dimensions={0} | all-to-all | bytes 720896 | tf_op jit(solution)/shard_map/all_to_all | solution.py:167
  87.1 3.1 %finish.1 = (f32[64,128]{1,0:T(8,128)}, f32[64,128]{1,0:T(8,128)}) custom-call(f32[64,128]{1,0:T(8,128)S(1)} %copy-done.2, f32[8,88,128]{2,1,0:T(8,128)S(1)} %all_to_all.17.t_ref), custom_call_target="tpu_custom_call" | custom-call | tf_op jit(solution)/shard_map/finish/pallas_call | solution.py:145
Async XLA Ops:
  0.6 1.6 %copy-start = (f32[32,16384]{1,0:T(8,128)S(1)}, f32[32,16384]{1,0:T(8,128)}, u32[]{:S(2)}) copy-start(f32[32,16384]{1,0:T(8,128)} %x_ref.3) | copy-start | bytes 6291460
  2.2 2.2 %copy-start.2 = (f32[64,128]{1,0:T(8,128)S(1)}, f32[64,128]{1,0:T(8,128)}, u32[]{:S(2)}) copy-start(f32[64,128]{1,0:T(8,128)} %s_ref.3) | copy-start | bytes 98308
  2.2 12.3 %copy-start.1 = (f32[32,16384]{1,0:T(8,128)S(1)}, f32[32,16384]{1,0:T(8,128)}, u32[]{:S(2)}) copy-start(f32[32,16384]{1,0:T(8,128)} %x_ref.3) | copy-start | bytes 6291460
  2.4 12.2 %collective-permute-start = (f32[32,8192]{1,0:T(8,128)S(1)}, f32[32,8192]{1,0:T(8,128)S(1)}, u32[]{:S(2)}, u32[]{:S(2)}) collective-permute-start(f32[32,8192]{1,0:T(8,128)S(1)} %away.1), channel_id=1, source_target_pairs={{0,4},{4,0},{1,5},{5,1},{2,6},{6,2},{3,7},{7,3},{8,12},{12,8},{9,1... | collective-permute-start | bytes 3145736 | tf_op jit(solution)/shard_map/ppermute | solution.py:162

commit v6 on v5

--- a/solution.py
+++ b/solution.py
@@ -14,6 +14,8 @@
 BIG = pltpu.CompilerParams(vmem_limit_bytes=32 * 2**20)
 F32 = jnp.float32
 PLACE = (0, 4, 2, 6, 1, 5, 3, 7)
+GROUP = (0, 1, 2, 3, 4, 5, 6, 7)
+NEAR = (0, 2, 4, 6, 1, 3, 5, 7)
 
 
 GRAM = 24
@@ -60,7 +62,7 @@
         o_ref[:, b * w : (b + 1) * w] = x_ref[:, pl.ds(col, w)]
 
 
-def sort_body(ny, at_ref, x_ref, a_ref, t_ref, o_ref):
+def sort_body(at_ref, x_ref, a_ref, t_ref, o_ref):
     ng = o_ref.shape[0]
     rows = x_ref.shape[0]
     _, tall, w = t_ref.shape
@@ -72,12 +74,12 @@
     other = pl.multiple_of((1 - c) * rows, rows)
     for g in range(ng):
         for zh in range(nh):
-            b = (zh * 2 + g // ny) * ny + g % ny
+            b = zh * ng + GROUP[g]
             base = zh * 2 * rows
             o_ref[g, pl.ds(base + mine, rows)] = x_ref[:, pl.ds(pl.multiple_of((2 * b + c) * w, w), w)]
             o_ref[g, pl.ds(base + other, rows)] = a_ref[:, b * w : (b + 1) * w]
     n = t_ref.shape[0]
-    sel = [t_ref[p, half:, :k] for p in range(n)]
+    sel = [t_ref[p, half:, :k] for p in NEAR]
     sel = jnp.concatenate([jnp.concatenate(sel[: n // 2], axis=0), jnp.concatenate(sel[n // 2 :], axis=0)], axis=1)
     gram = jnp.sum(t_ref[:, :half], axis=0)
     tail = jnp.concatenate([sel, gram], axis=0)
@@ -149,20 +151,18 @@
 
 def local(sketch, slab):
     k, sk = sketch.shape
-    nl, ny, nc, nx = (lax.axis_size(a) for a in ("zl", "y", "c", "x"))
-    nh = len(PLACE)
+    nh, ng, nc, nx = len(PLACE), len(GROUP), 2, 4
     rows, cols = slab.shape
-    ng = nl * ny
     out = cols // (nh * ng * nc)
     at = lax.axis_index("c").astype(jnp.int32)[None]
 
     (own,) = call(functools.partial(pack_body, 1.0 / (sk * nh * ng * nc * nx)), [(nc * nx, GRAM + SUB, out)], "pack", sketch)
-    own = lax.all_to_all(own, ("c", "x"), 0, 0, tiled=True)
+    own = lax.all_to_all(own, ("x1", "x0", "c"), 0, 0, tiled=True)
     (away,) = call(functools.partial(away_body, out), [(rows, cols // nc)], "away", at, slab)
     away = lax.ppermute(away, "c", [(0, 1), (1, 0)])
     rows *= nc
-    (sent,) = call(functools.partial(sort_body, ny), [(ng, nh * rows + rows // 2 + GRAM, out)], "sort", at, slab, away, own)
-    sent = lax.all_to_all(sent, ("zl", "y"), 0, 0, tiled=True)
+    (sent,) = call(sort_body, [(ng, nh * rows + rows // 2 + GRAM, out)], "sort", at, slab, away, own)
+    sent = lax.all_to_all(sent, ("zl", "y1", "y0"), 0, 0, tiled=True)
     (part,) = call(functools.partial(project_body, rows), [(nh, k + GRAM, out)], "project", sent)
     part = lax.all_to_all(part, ("z2", "z1", "z0"), 0, 0, tiled=True)
     scale = 1.0 / (rows * nh * ng) ** 0.5
@@ -171,13 +171,12 @@
 
 
 def solution(mesh):
-    nx = mesh.shape["narrow"]
-    grid = Mesh(mesh.devices.reshape(2, 2, 2, 2, 4, 2, nx), ("z0", "z1", "z2", "zl", "y", "c", "x"))
-    wide = ("z0", "z1", "z2", "zl", "y", "c")
+    wide, narrow = ("z0", "z1", "z2", "zl", "y1", "y0", "c"), ("x1", "x0")
+    grid = Mesh(mesh.devices.reshape((2,) * 9), wide + narrow)
     return jax.shard_map(
         local,
         mesh=grid,
-        in_specs=(P(None, (*wide, "x")), P(wide, "x")),
-        out_specs=(P(None, (*wide, "x")), P(None, ("x", *wide))),
+        in_specs=(P(None, wide + narrow), P(wide, narrow)),
+        out_specs=(P(None, wide + narrow), P(None, narrow + wide)),
         check_vma=False,
     )

time: 90.4 us -> 90.1 us (level)
  the two profiles are of different devices: /device:TPU:32 before, /device:TPU:64 now
where the time goes in v6:
time: 90.1 us; the launch traced here: 89.8 us
  blocking collectives  80.4 us (89%)
  Pallas kernels  5.07 us (6%)
  starting transfers between devices  2.05 us (2%)
  local copies, waits for them, and re-layouts  1.59 us (2%)
    all_to_all x1, blocking collectives, local(): part = lax.all_to_all(part, ('z2', 'z1', 'z0'), 0, 0, tiled=True)  35.3 us
    all_to_all x1, blocking collectives, local(): sent = lax.all_to_all(sent, ('zl', 'y1', 'y0'), 0, 0, tiled=True)  34.8 us
    all_to_all x1, blocking collectives, local(): own = lax.all_to_all(own, ('x1', 'x0', 'c'), 0, 0, tiled=True)  10.4 us
    pallas_call x5, Pallas kernels, call(): pl.pallas_call(body, out_shape=shapes, in_specs=where, out_specs=[VMEM] *...  5.07 us
    ppermute x1, starting transfers between devices, local(): away = lax.ppermute(away, 'c', [(0, 1), (1, 0)])  2.05 us
  transfers between devices with their start and end apart: 1, of which 0 were waited for; matrix products, arithmetic and copies ran while one was open for 0% of the time, Pallas kernels for 0%

profile of v6, /device:TPU:64, one launch (start us, length us, event | category | flops | bytes accessed | tf_op | source)
XLA Modules:
  0.0 89.8 jit_solution(10805701512912200559)
XLA Ops:
  0.6 0.0 copy-start
  0.6 1.6 %copy-done = f32[32,16384]{1,0:T(8,128)S(1)} copy-done((f32[32,16384]{1,0:T(8,128)S(1)}, f32[32,16384]{1,0:T(8,128)}, u32[]{:S(2)}) %copy-start) | copy-done | bytes 2097176
  2.2 0.0 copy-start.2
  2.2 0.0 copy-start.1
  2.2 0.1 away.1
  2.4 2.1 %collective-permute-start = (f32[32,8192]{1,0:T(8,128)S(1)}, f32[32,8192]{1,0:T(8,128)S(1)}, u32[]{:S(2)}, u32[]{:S(2)}) collective-permute-start(f32[32,8192]{1,0:T(8,128)S(1)} %away.1), channel_id=1, source_target_pairs={{0,4},{4,0},{1,5},{5,1},{2,6},{6,2},{3,7},{7,3},{8,12},{12,8},{9,1... | collective-permute-start | bytes 3145736 | tf_op jit(solution)/shard_map/ppermute | solution.py:162
  4.4 0.0 copy-done.2
  4.4 0.3 pack.1
  4.7 10.4 %all_to_all.15.t_ref = f32[8,32,128]{2,1,0:T(8,128)S(1)} all-to-all(f32[8,32,128]{2,1,0:T(8,128)S(1)} %pack.1), channel_id=1, replica_groups=mesh['z0'=2,'z1'=2,'z2'=2,'zl'=2,'y1'=2,'y0'=2,'c'=2,'x1'=2,'x0'=2] {'x1..., dimensions={0} | all-to-all | bytes 262144 | tf_op jit(solution)/shard_map/all_to_all | solution.py:160
  15.1 0.0 collective-permute-done.a_ref
  15.1 0.0 copy-done.1
  15.1 0.2 sort.1
  15.3 34.8 %all_to_all.16.t_ref = f32[8,568,128]{2,1,0:T(8,128)S(1)} all-to-all(f32[8,568,128]{2,1,0:T(8,128)S(1)} %sort.1), channel_id=1, replica_groups=mesh['z0'=2,'z1'=2,'z2'=2,'zl'=2,'y1'=2,'y0'=2,'c'=2,'x1'=2,'x0'=2] {'zl..., dimensions={0} | all-to-all | bytes 4653056 | tf_op jit(solution)/shard_map/all_to_all | solution.py:165
  50.1 1.4 %project.1 = f32[8,88,128]{2,1,0:T(8,128)S(1)} custom-call(f32[8,568,128]{2,1,0:T(8,128)S(1)} %all_to_all.16.t_ref), custom_call_target="tpu_custom_call" | custom-call | tf_op jit(solution)/shard_map/project/pallas_call | solution.py:147
  51.5 35.3 %all_to_all.17.t_ref = f32[8,88,128]{2,1,0:T(8,128)S(1)} all-to-all(f32[8,88,128]{2,1,0:T(8,128)S(1)} %project.1), channel_id=1, replica_groups=mesh['z0'=2,'z1'=2,'z2'=2,'zl'=2,'y1'=2,'y0'=2,'c'=2,'x1'=2,'x0'=2] {'z2..., dimensions={0} | all-to-all | bytes 720896 | tf_op jit(solution)/shard_map/all_to_all | solution.py:167
  86.8 3.1 %finish.1 = (f32[64,128]{1,0:T(8,128)}, f32[64,128]{1,0:T(8,128)}) custom-call(f32[64,128]{1,0:T(8,128)S(1)} %copy-done.2, f32[8,88,128]{2,1,0:T(8,128)S(1)} %all_to_all.17.t_ref), custom_call_target="tpu_custom_call" | custom-call | tf_op jit(solution)/shard_map/finish/pallas_call | solution.py:147
Async XLA Ops:
  0.6 1.6 %copy-start = (f32[32,16384]{1,0:T(8,128)S(1)}, f32[32,16384]{1,0:T(8,128)}, u32[]{:S(2)}) copy-start(f32[32,16384]{1,0:T(8,128)} %x_ref.3) | copy-start | bytes 6291460
  2.2 2.2 %copy-start.2 = (f32[64,128]{1,0:T(8,128)S(1)}, f32[64,128]{1,0:T(8,128)}, u32[]{:S(2)}) copy-start(f32[64,128]{1,0:T(8,128)} %s_ref.3) | copy-start | bytes 98308
  2.2 12.9 %copy-start.1 = (f32[32,16384]{1,0:T(8,128)S(1)}, f32[32,16384]{1,0:T(8,128)}, u32[]{:S(2)}) copy-start(f32[32,16384]{1,0:T(8,128)} %x_ref.3) | copy-start | bytes 6291460
  2.4 12.7 %collective-permute-start = (f32[32,8192]{1,0:T(8,128)S(1)}, f32[32,8192]{1,0:T(8,128)S(1)}, u32[]{:S(2)}, u32[]{:S(2)}) collective-permute-start(f32[32,8192]{1,0:T(8,128)S(1)} %away.1), channel_id=1, source_target_pairs={{0,4},{4,0},{1,5},{5,1},{2,6},{6,2},{3,7},{7,3},{8,12},{12,8},{9,1... | collective-permute-start | bytes 3145736 | tf_op jit(solution)/shard_map/ppermute | solution.py:162

commit v7 on v6

--- a/solution.py
+++ b/solution.py
@@ -14,7 +14,7 @@
 BIG = pltpu.CompilerParams(vmem_limit_bytes=32 * 2**20)
 F32 = jnp.float32
 PLACE = (0, 4, 2, 6, 1, 5, 3, 7)
-GROUP = (0, 1, 2, 3, 4, 5, 6, 7)
+GROUP = (0, 2, 1, 3, 4, 6, 5, 7)
 NEAR = (0, 2, 4, 6, 1, 3, 5, 7)
 
 
@@ -162,7 +162,7 @@
     away = lax.ppermute(away, "c", [(0, 1), (1, 0)])
     rows *= nc
     (sent,) = call(sort_body, [(ng, nh * rows + rows // 2 + GRAM, out)], "sort", at, slab, away, own)
-    sent = lax.all_to_all(sent, ("zl", "y1", "y0"), 0, 0, tiled=True)
+    sent = lax.all_to_all(sent, ("zl", "y0", "y1"), 0, 0, tiled=True)
     (part,) = call(functools.partial(project_body, rows), [(nh, k + GRAM, out)], "project", sent)
     part = lax.all_to_all(part, ("z2", "z1", "z0"), 0, 0, tiled=True)
     scale = 1.0 / (rows * nh * ng) ** 0.5

time: 90.1 us -> 89.8 us (level)
  the two profiles are of different devices: /device:TPU:64 before, /device:TPU:32 now
where the time goes in v7:
time: 89.8 us; the launch traced here: 89.5 us
  blocking collectives  80 us (89%)
  Pallas kernels  5.11 us (6%)
  starting transfers between devices  2.05 us (2%)
  local copies, waits for them, and re-layouts  1.59 us (2%)
    all_to_all x1, blocking collectives, local(): part = lax.all_to_all(part, ('z2', 'z1', 'z0'), 0, 0, tiled=True)  35.5 us
    all_to_all x1, blocking collectives, local(): sent = lax.all_to_all(sent, ('zl', 'y0', 'y1'), 0, 0, tiled=True)  34.2 us
    all_to_all x1, blocking collectives, local(): own = lax.all_to_all(own, ('x1', 'x0', 'c'), 0, 0, tiled=True)  10.4 us
    pallas_call x5, Pallas kernels, call(): pl.pallas_call(body, out_shape=shapes, in_specs=where, out_specs=[VMEM] *...  5.11 us
    ppermute x1, starting transfers between devices, local(): away = lax.ppermute(away, 'c', [(0, 1), (1, 0)])  2.05 us
  transfers between devices with their start and end apart: 1, of which 0 were waited for; matrix products, arithmetic and copies ran while one was open for 0% of the time, Pallas kernels for 0%

profile of v7, /device:TPU:32, one launch (start us, length us, event | category | flops | bytes accessed | tf_op | source)
XLA Modules:
  0.0 89.5 jit_solution(3150027571756365138)
XLA Ops:
  0.6 0.0 copy-start
  0.6 1.6 %copy-done = f32[32,16384]{1,0:T(8,128)S(1)} copy-done((f32[32,16384]{1,0:T(8,128)S(1)}, f32[32,16384]{1,0:T(8,128)}, u32[]{:S(2)}) %copy-start) | copy-done | bytes 2097176
  2.2 0.0 copy-start.2
  2.2 0.0 copy-start.1
  2.2 0.1 away.1
  2.4 2.1 %collective-permute-start = (f32[32,8192]{1,0:T(8,128)S(1)}, f32[32,8192]{1,0:T(8,128)S(1)}, u32[]{:S(2)}, u32[]{:S(2)}) collective-permute-start(f32[32,8192]{1,0:T(8,128)S(1)} %away.1), channel_id=1, source_target_pairs={{0,4},{4,0},{1,5},{5,1},{2,6},{6,2},{3,7},{7,3},{8,12},{12,8},{9,1... | collective-permute-start | bytes 3145736 | tf_op jit(solution)/shard_map/ppermute | solution.py:162
  4.4 0.0 copy-done.2
  4.4 0.3 pack.1
  4.7 10.4 %all_to_all.15.t_ref = f32[8,32,128]{2,1,0:T(8,128)S(1)} all-to-all(f32[8,32,128]{2,1,0:T(8,128)S(1)} %pack.1), channel_id=1, replica_groups=mesh['z0'=2,'z1'=2,'z2'=2,'zl'=2,'y1'=2,'y0'=2,'c'=2,'x1'=2,'x0'=2] {'x1..., dimensions={0} | all-to-all | bytes 262144 | tf_op jit(solution)/shard_map/all_to_all | solution.py:160
  15.1 0.0 collective-permute-done.a_ref
  15.1 0.0 copy-done.1
  15.1 0.3 sort.1
  15.4 34.2 %all_to_all.16.t_ref = f32[8,568,128]{2,1,0:T(8,128)S(1)} all-to-all(f32[8,568,128]{2,1,0:T(8,128)S(1)} %sort.1), channel_id=1, replica_groups=mesh['z0'=2,'z1'=2,'z2'=2,'zl'=2,'y1'=2,'y0'=2,'c'=2,'x1'=2,'x0'=2] {'zl..., dimensions={0} | all-to-all | bytes 4653056 | tf_op jit(solution)/shard_map/all_to_all | solution.py:165
  49.6 1.4 %project.1 = f32[8,88,128]{2,1,0:T(8,128)S(1)} custom-call(f32[8,568,128]{2,1,0:T(8,128)S(1)} %all_to_all.16.t_ref), custom_call_target="tpu_custom_call" | custom-call | tf_op jit(solution)/shard_map/project/pallas_call | solution.py:147
  50.9 35.5 %all_to_all.17.t_ref = f32[8,88,128]{2,1,0:T(8,128)S(1)} all-to-all(f32[8,88,128]{2,1,0:T(8,128)S(1)} %project.1), channel_id=1, replica_groups=mesh['z0'=2,'z1'=2,'z2'=2,'zl'=2,'y1'=2,'y0'=2,'c'=2,'x1'=2,'x0'=2] {'z2..., dimensions={0} | all-to-all | bytes 720896 | tf_op jit(solution)/shard_map/all_to_all | solution.py:167
  86.4 3.1 %finish.1 = (f32[64,128]{1,0:T(8,128)}, f32[64,128]{1,0:T(8,128)}) custom-call(f32[64,128]{1,0:T(8,128)S(1)} %copy-done.2, f32[8,88,128]{2,1,0:T(8,128)S(1)} %all_to_all.17.t_ref), custom_call_target="tpu_custom_call" | custom-call | tf_op jit(solution)/shard_map/finish/pallas_call | solution.py:147
Async XLA Ops:
  0.6 1.6 %copy-start = (f32[32,16384]{1,0:T(8,128)S(1)}, f32[32,16384]{1,0:T(8,128)}, u32[]{:S(2)}) copy-start(f32[32,16384]{1,0:T(8,128)} %x_ref.3) | copy-start | bytes 6291460
  2.2 2.2 %copy-start.2 = (f32[64,128]{1,0:T(8,128)S(1)}, f32[64,128]{1,0:T(8,128)}, u32[]{:S(2)}) copy-start(f32[64,128]{1,0:T(8,128)} %s_ref.3) | copy-start | bytes 98308
  2.2 12.9 %copy-start.1 = (f32[32,16384]{1,0:T(8,128)S(1)}, f32[32,16384]{1,0:T(8,128)}, u32[]{:S(2)}) copy-start(f32[32,16384]{1,0:T(8,128)} %x_ref.3) | copy-start | bytes 6291460
  2.4 12.7 %collective-permute-start = (f32[32,8192]{1,0:T(8,128)S(1)}, f32[32,8192]{1,0:T(8,128)S(1)}, u32[]{:S(2)}, u32[]{:S(2)}) collective-permute-start(f32[32,8192]{1,0:T(8,128)S(1)} %away.1), channel_id=1, source_target_pairs={{0,4},{4,0},{1,5},{5,1},{2,6},{6,2},{3,7},{7,3},{8,12},{12,8},{9,1... | collective-permute-start | bytes 3145736 | tf_op jit(solution)/shard_map/ppermute | solution.py:162
